TPU v7x, 32 devices: a whole 2x2x4 slice. The times are simulated.
32 devices in a mesh: groups: 2 (over x), replica: 4 (over y, core), tensor: 4 (over z).
Axes of the slice: x: 2, y: 2, z: 4, core: 2. Of those that a mesh axis runs over, the one named last changes fastest.
Arguments:
- queries: bfloat16 [256, 32, 8192], P(('groups', 'replica'), None, 'tensor'), parts along dimension 0, may hold values from -15 to 15
- suffix_key_value: bfloat16 [256, 32, 8, 256], P(('groups', 'replica'), None, 'tensor'), parts along dimension 0, may hold values from -6 to 6
- kv_pool: bfloat16 [512, 64, 8, 256], P(('groups', 'replica'), None, 'tensor'), parts along dimension 0, may hold values from -7 to 7
- page_table: int32 [256, 16], P(('groups', 'replica')), parts along dimension 0, may hold values from 0 to 63
- lengths: int32 [256], P(('groups', 'replica')), parts along dimension 0, may hold values from 1 to 32, 2048 in all
- destination: int32 [256, 1], P(('groups', 'replica')), parts along dimension 0, may hold values from 0 to 3; in each aligned block of 32 rows (0 to 31, 32 to 63, ...) at most 9 rows name the same one
Outputs:
- context: bfloat16 [256, 32, 8192], P(('groups', 'replica'), None, 'tensor'), parts along dimension 0
There are 2 independent parts, one for each index of `groups`. A program takes and returns all parts, laid end to end along the dimension named above; each array names one. Nothing has to cross between parts.
Inputs may be any that keep to these rules, and one draw needn't show every extreme that they name: `page_table`: entries name pages of the destination replica's pool; pages may repeat. In each part of groups the lengths sum to 2048, and some request has all 32 tokens live. Among the requests of one replica at most 9 name the same destination, and in every draw some replica sends exactly 9 to one destination.
All inputs are finite; a program needn't handle non-finite values.
Results may differ from a plain program's by a relative error of at most 0.0049.
Values may be sent and summed in bfloat16 or wider, within the bound.
No kernel may reach another device: no remote copies, remote signals or barrier semaphores. Data moves between devices by JAX's collectives and lax.ppermute only.
A program may use at most 128 MiB of HBM per device.

v0:
```python
import functools
import math

import jax
import jax.numpy as jnp
from jax import lax
from jax.experimental import pallas as pl
from jax.experimental.pallas import tpu as pltpu
from jax.sharding import PartitionSpec as P

BIG = 1 << 14
STAT = 128
VMEM_LIMIT = 60 << 20


def cost(microseconds):
    return pl.CostEstimate(
        flops=int(microseconds * 1.1e9), bytes_accessed=1 << 10, transcendentals=0
    )


def vspec():
    return pl.BlockSpec(memory_space=pltpu.VMEM)


def sspec():
    return pl.BlockSpec(memory_space=pltpu.SMEM)


def anyspec():
    return pl.BlockSpec(memory_space=pl.ANY)


def shift_of(target, chips):
    here = lax.axis_index("replica") >> 1
    step = (target >> 1) - here
    return jnp.where(step < 0, step + chips, step)


def flow(chips, requests, way, first, rows, size_of, to_of, todo, begin):
    def listing(i, carry):
        count, row = carry
        size = jnp.where(shift_of(to_of(i), chips) == way, size_of(i), 0)
        low = jnp.maximum(row, first)
        high = jnp.minimum(row + size, first + rows)
        todo[count] = i
        begin[count] = row - first
        return count + (high > low).astype(jnp.int32), row + size

    return lax.fori_loop(0, requests, listing, (jnp.int32(0), jnp.int32(0)), unroll=8)[0]


def pack_kernel(
    chips, chunk, requests, len_ref, dst_ref, q_ref, out_ref, tiles, hot, todo, begin, sem
):
    way, first, rows = chunk
    many, steps, width = tiles.shape[1:]
    count = flow(
        chips, requests, way, first, rows, lambda i: len_ref[i], lambda i: dst_ref[i], todo, begin
    )
    blocks = (count + many - 1) // many

    def take(j, slot, u):
        i = todo[jnp.minimum(j * many + u, count - 1)]
        return pltpu.make_async_copy(q_ref.at[i], tiles.at[slot, u], sem.at[slot, u])

    def start(j, slot):
        for u in range(many):
            take(j, slot, u).start()

    @pl.when(count > 0)
    def _():
        start(0, 0)

    @pl.when(count == 0)
    def _():
        out_ref[...] = jnp.zeros_like(out_ref)

    def step(j, carry):
        slot = lax.rem(j, 2)

        @pl.when(j + 1 < blocks)
        def _():
            start(j + 1, 1 - slot)

        row = lax.broadcasted_iota(jnp.int32, (rows, many * steps), 0)
        lane = lax.broadcasted_iota(jnp.int32, (1, many * steps), 1)
        place = jnp.full((1, many * steps), -1, jnp.int32)
        for u in range(many):
            n = jnp.minimum(j * many + u, count - 1)
            size = jnp.where(j * many + u < count, len_ref[todo[n]], 0)
            token = lane - u * steps
            place = jnp.where((token >= 0) & (token < size), begin[n] + token, place)
        hot[...] = jnp.where(row == place, 1.0, 0.0).astype(jnp.bfloat16)
        for u in range(many):
            take(j, slot, u).wait()
        block = tiles[slot].reshape(many * steps, width)
        rows_of = jnp.dot(hot[...], block, preferred_element_type=jnp.float32).astype(jnp.bfloat16)

        @pl.when(j == 0)
        def _():
            out_ref[...] = rows_of

        @pl.when(j > 0)
        def _():
            out_ref[...] += rows_of

        return carry

    lax.fori_loop(0, blocks, step, 0)


def pack(queries, lengths, target, chips, chunk):
    requests, steps, width = queries.shape
    rows = chunk[2]
    many = 16
    return pl.pallas_call(
        functools.partial(pack_kernel, chips, chunk, requests),
        in_specs=[sspec(), sspec(), anyspec()],
        out_specs=vspec(),
        out_shape=jax.ShapeDtypeStruct((rows, width), jnp.bfloat16),
        scratch_shapes=[
            pltpu.VMEM((2, many, steps, width), jnp.bfloat16),
            pltpu.VMEM((rows, many * steps), jnp.bfloat16),
            pltpu.SMEM((requests + 1,), jnp.int32),
            pltpu.SMEM((requests + 1,), jnp.int32),
            pltpu.SemaphoreType.DMA((2, many)),
        ],
        compiler_params=pltpu.CompilerParams(vmem_limit_bytes=VMEM_LIMIT),
        cost_estimate=cost(1),
        name="pack",
    )(lengths, target, queries)


def nt_dot(a, b):
    return lax.dot_general(a, b, (((1,), (1,)), ((), ())), preferred_element_type=jnp.float32)


def with_ones(values):
    return jnp.concatenate([values, jnp.ones_like(values)], axis=1)


def stacked(q, k, group, head):
    return jnp.concatenate(
        [q[:, (k * group + g) * head : (k * group + g + 1) * head] for g in range(group)], axis=0
    )


def attend(items, dims, window, pool, scores):
    requests, steps, kv, group, head, pages = dims
    coeff = 1.0 / math.sqrt(head)
    rows = group * window
    per = pool.shape[2]
    count = 4 if pages % 4 == 0 else 1
    work = [(n, k) for n in range(len(items)) for k in range(kv)]
    s_refs = dict(zip(work, scores[: len(work)]))
    p_refs = dict(zip(work, scores[len(work) :]))
    if items[0][2] is not None:
        key = lax.broadcasted_iota(jnp.int32, (window, steps), 1)
        token = lax.broadcasted_iota(jnp.int32, (window, steps), 0)
        causal = jnp.where(key <= token, 0.0, -1e30)
        causal = jnp.concatenate([causal] * group, axis=0)
    nears = {}
    for n, k in work:
        q, ids, suffix = items[n]
        qk = stacked(q, k, group, head)
        for p in range(0, pages, count):
            keys = jnp.concatenate([pool[i, k, :, 0:head] for i in ids[p : p + count]], axis=0)
            s_refs[n, k][0:rows, p * per : (p + count) * per] = nt_dot(qk, keys)
        if suffix is not None:
            nears[n, k] = nt_dot(qk, suffix[k, :, 0:head]) + causal
    tops = {}
    for n, k in work:
        found = []
        for r in range(0, rows, 16):
            score = s_refs[n, k][r : r + 16, :]
            top = jnp.max(score, axis=1, keepdims=True)
            if (n, k) in nears:
                near = nears[n, k][r : r + 16]
                top = jnp.maximum(top, jnp.max(near, axis=1, keepdims=True))
            p_refs[n, k][r : r + 16, :] = jnp.exp((score - top) * coeff).astype(jnp.bfloat16)
            found.append(top)
        tops[n, k] = jnp.concatenate(found, axis=0)
    mixes = {}
    for n, k in work:
        q, ids, suffix = items[n]
        values = jnp.concatenate([pool[i, k, :, head : 2 * head] for i in ids], axis=0)
        mixed = jnp.dot(
            p_refs[n, k][0:rows, :], with_ones(values), preferred_element_type=jnp.float32
        )
        if suffix is not None:
            weight = jnp.exp((nears[n, k] - tops[n, k]) * coeff).astype(jnp.bfloat16)
            mixed += jnp.dot(
                weight,
                with_ones(suffix[k, :, head : 2 * head]),
                preferred_element_type=jnp.float32,
            )
        mixes[n, k] = mixed
    results = [[None] * kv for _ in items]
    for n, k in work:
        total = mixes[n, k][:, head : 2 * head]
        results[n][k] = (mixes[n, k][:, 0:head] * inverse(total), tops[n, k] * coeff, total)
    return results


def inverse(total):
    share = pl.reciprocal(total, approx=True)
    return share * (2.0 - total * share)


def split_stat(values, group, window):
    lane = lax.broadcasted_iota(jnp.int32, (window, STAT), 1)
    count = len(values) * group
    assert count & (count - 1) == 0
    which = lane & (count - 1)
    level = jnp.zeros((window, STAT), jnp.float32)
    total = jnp.ones((window, STAT), jnp.float32)
    for k, (_, top, weight) in enumerate(values):
        for g in range(group):
            here = which == k * group + g
            level = jnp.where(here, top[g * window : (g + 1) * window], level)
            total = jnp.where(here, weight[g * window : (g + 1) * window, 0:STAT], total)
    stat = level + jnp.log(total)
    high = stat.astype(jnp.bfloat16).astype(jnp.float32)
    rest = stat - high
    middle = rest.astype(jnp.bfloat16).astype(jnp.float32)
    low = rest - middle
    stat = jnp.where(lane < count, high, jnp.where(lane < 2 * count, middle, low))
    return jnp.where(lane < 3 * count, stat, 0.0)


def load_pools(own_ref, sib_ref, pool, sem):
    count = own_ref.shape[0]
    return (
        pltpu.make_async_copy(own_ref, pool.at[pl.ds(0, count)], sem.at[0]),
        pltpu.make_async_copy(sib_ref, pool.at[pl.ds(count, count)], sem.at[1]),
    )


def arrange(requests, classes, class_of, keys, counts, todo):
    for c in range(classes + 1):
        counts[c] = 0

    def tally(i, carry):
        c = class_of(i)
        keys[i] = c
        counts[c + 1] = counts[c + 1] + 1
        return carry

    lax.fori_loop(0, requests, tally, 0, unroll=8)
    for c in range(classes):
        counts[c + 1] = counts[c + 1] + counts[c]

    def place(i, carry):
        c = keys[i]
        spot = counts[c]
        todo[spot] = i
        counts[c] = spot + 1
        return carry

    lax.fori_loop(0, requests, place, 0, unroll=8)


def score_scratch(kv, keys, rows):
    return [pltpu.VMEM((rows, keys), jnp.float32) for _ in range(2 * kv)] + [
        pltpu.VMEM((rows, keys), jnp.bfloat16) for _ in range(2 * kv)
    ]


BATCH = 4


def near_kernel(
    chips, dims, len_ref, dst_ref, q_ref, suf_ref, ctx_ref, stat_ref, q_buf, o_buf, todo, q_sem, o_sem
):
    requests, steps, kv, group, head, pages = dims
    coeff = 1.0 / math.sqrt(head)

    def listing(i, count):
        todo[count] = i
        return count + (shift_of(dst_ref[i], chips) != 0).astype(jnp.int32)

    count = lax.fori_loop(0, requests, listing, jnp.int32(0), unroll=8)
    blocks = (count + BATCH - 1) // BATCH

    def each(block, make, act):
        for u in range(BATCH):

            @pl.when(block * BATCH + u < count)
            def _():
                getattr(make(block, u), act)()

    def take(block, u):
        slot = lax.rem(block, 2)
        i = todo[block * BATCH + u]
        return pltpu.make_async_copy(q_ref.at[i], q_buf.at[slot, u], q_sem.at[slot, u])

    def give(block, u):
        slot = lax.rem(block, 2)
        i = todo[block * BATCH + u]
        return pltpu.make_async_copy(o_buf.at[slot, u], ctx_ref.at[i], o_sem.at[slot, u])

    each(0, take, "start")
    stat_ref[...] = jnp.zeros_like(stat_ref)
    key = lax.broadcasted_iota(jnp.int32, (steps, BATCH * steps), 1)
    token = lax.broadcasted_iota(jnp.int32, (steps, BATCH * steps), 0)
    masks = []
    for u in range(BATCH):
        mine = (key >= u * steps) & (key - u * steps <= token)
        masks.append(jnp.concatenate([jnp.where(mine, 0.0, -1e30)] * group, axis=0))

    def step(block, carry):
        slot = lax.rem(block, 2)
        each(block + 1, take, "start")
        @pl.when(block >= 2)
        def _():
            each(block - 2, give, "wait")

        each(block, take, "wait")
        picked = [todo[jnp.minimum(block * BATCH + u, count - 1)] for u in range(BATCH)]
        found = []
        for k in range(kv):
            keys = jnp.concatenate([suf_ref[i, k, :, 0:head] for i in picked], axis=0)
            found.append(
                [
                    nt_dot(stacked(q_buf[slot, u], k, group, head), keys) + masks[u]
                    for u in range(BATCH)
                ]
            )
        tops = [[jnp.max(score, axis=1, keepdims=True) for score in scores] for scores in found]
        for u in range(BATCH):
            i = picked[u]
            live = lax.broadcasted_iota(jnp.int32, (steps, head), 0) < len_ref[i]
            values = []
            for k in range(kv):
                rows = jnp.concatenate([suf_ref[n, k, :, head : 2 * head] for n in picked], axis=0)
                weight = jnp.exp((found[k][u] - tops[k][u]) * coeff).astype(jnp.bfloat16)
                mixed = jnp.dot(weight, with_ones(rows), preferred_element_type=jnp.float32)
                total = mixed[:, head : 2 * head]
                mixed = mixed[:, 0:head] * inverse(total)
                values.append((None, tops[k][u] * coeff, total))
                for g in range(group):
                    h = k * group + g
                    part = jnp.where(live, mixed[g * steps : (g + 1) * steps], 0.0)
                    o_buf[slot, u, :, h * head : (h + 1) * head] = part.astype(jnp.bfloat16)
            stat = split_stat(values, group, steps).astype(jnp.bfloat16)

            @pl.when(block * BATCH + u < count)
            def _():
                stat_ref[i] = stat

        each(block, give, "start")
        return carry

    lax.fori_loop(0, blocks, step, 0)

    def drain(block, carry):
        each(block, give, "wait")
        return carry

    lax.fori_loop(jnp.maximum(blocks - 2, 0), blocks, drain, 0)


def near_part(queries, suffix, lengths, target, dims, chips):
    requests, steps, width = queries.shape
    return pl.pallas_call(
        functools.partial(near_kernel, chips, dims),
        in_specs=[sspec(), sspec(), anyspec(), vspec()],
        out_specs=[anyspec(), vspec()],
        out_shape=[
            jax.ShapeDtypeStruct(queries.shape, jnp.bfloat16),
            jax.ShapeDtypeStruct((requests, steps, STAT), jnp.bfloat16),
        ],
        scratch_shapes=[
            pltpu.VMEM((2, BATCH, steps, width), jnp.bfloat16),
            pltpu.VMEM((2, BATCH, steps, width), jnp.bfloat16),
            pltpu.SMEM((requests + 1,), jnp.int32),
            pltpu.SemaphoreType.DMA((2, BATCH)),
            pltpu.SemaphoreType.DMA((2, BATCH)),
        ],
        compiler_params=pltpu.CompilerParams(vmem_limit_bytes=VMEM_LIMIT),
        cost_estimate=cost(2),
        name="near",
    )(lengths, target, queries, suffix)


DEPTH = 3


def local_kernel(
    chips, dims, len_ref, dst_ref, table_ref, q_ref, suf_ref, own_ref, sib_ref, old_ref,
    ctx_ref, pool, q_buf, o_buf, todo, keys, ends, sem, q_sem, o_sem, *scores,
):
    requests, steps, kv, group, head, pages = dims
    core = lax.rem(lax.axis_index("replica"), 2)
    held = own_ref.shape[0]
    quarter = steps // 4
    load_own, load_sib = load_pools(own_ref, sib_ref, pool, sem)
    load_own.start()
    load_sib.start()

    def class_of(i):
        need = (len_ref[i] + quarter - 1) // quarter
        mine = jnp.where(lax.rem(dst_ref[i], 2) == core, 0, 4) + 4 - need
        return jnp.where(shift_of(dst_ref[i], chips) == 0, mine, 8)

    arrange(requests, 9, class_of, keys, ends, todo)
    owned, count = ends[3], ends[7]
    pairs = (count + 1) // 2

    def each(pair, make, act):
        for u in range(2):

            @pl.when(2 * pair + u < count)
            def _():
                getattr(make(pair, u), act)()

    def take(pair, u):
        slot = 2 * lax.rem(pair, DEPTH) + u
        return pltpu.make_async_copy(q_ref.at[todo[2 * pair + u]], q_buf.at[slot], q_sem.at[slot])

    def give(pair, u):
        slot = 2 * lax.rem(pair, DEPTH) + u
        return pltpu.make_async_copy(o_buf.at[slot], ctx_ref.at[todo[2 * pair + u]], o_sem.at[slot])

    for ahead in range(DEPTH - 1):
        each(ahead, take, "start")

    def compute(pair, picked, window):
        slots = [2 * lax.rem(pair, DEPTH) + u for u in range(2)]
        items = []
        for u, i in enumerate(picked):
            shift = jnp.where(lax.rem(dst_ref[i], 2) == core, 0, held)
            ids = [table_ref[i, p] + shift for p in range(pages)]
            items.append((q_buf[slots[u], 0:window, :], ids, suf_ref.at[i]))
        found = attend(items, dims, window, pool, scores)
        for u, i in enumerate(picked):
            live = lax.broadcasted_iota(jnp.int32, (window, head), 0) < len_ref[i]
            for k in range(kv):
                for g in range(group):
                    h = k * group + g
                    part = found[u][k][0][g * window : (g + 1) * window]
                    part = jnp.where(live, part, 0.0).astype(jnp.bfloat16)
                    o_buf[slots[u], 0:window, h * head : (h + 1) * head] = part
            if window < steps:
                o_buf[slots[u], window:steps, :] = jnp.zeros(
                    (steps - window, o_buf.shape[2]), jnp.bfloat16
                )

    load_own.wait()

    @pl.when(owned == count)
    def _():
        load_sib.wait()

    def step(pair, carry):
        each(pair + DEPTH - 1, take, "start")

        @pl.when(pair >= DEPTH)
        def _():
            each(pair - DEPTH, give, "wait")

        @pl.when((owned < count) & (pair == owned // 2))
        def _():
            load_sib.wait()

        each(pair, take, "wait")
        picked = [todo[2 * pair], todo[jnp.minimum(2 * pair + 1, count - 1)]]
        size = jnp.maximum(len_ref[picked[0]], len_ref[picked[1]])
        need = (size + quarter - 1) // quarter
        for quarters in (1, 2, 3, 4):

            @pl.when(need == quarters)
            def _():
                compute(pair, picked, quarter * quarters)

        each(pair, give, "start")
        return carry

    lax.fori_loop(0, pairs, step, 0)

    def drain(pair, carry):
        each(pair, give, "wait")
        return carry

    lax.fori_loop(jnp.maximum(pairs - DEPTH, 0), pairs, drain, 0)


def local(queries, suffix, own, sib, ctx, table, lengths, target, dims, chips):
    requests, steps, kv, group, head, pages = dims
    width = queries.shape[2]
    held = own.shape[0]
    return pl.pallas_call(
        functools.partial(local_kernel, chips, dims),
        in_specs=[sspec(), sspec(), sspec(), anyspec(), vspec()] + [anyspec()] * 3,
        out_specs=anyspec(),
        out_shape=jax.ShapeDtypeStruct(queries.shape, jnp.bfloat16),
        input_output_aliases={7: 0},
        scratch_shapes=[
            pltpu.VMEM((2 * held,) + own.shape[1:], jnp.bfloat16),
            pltpu.VMEM((2 * DEPTH, steps, width), jnp.bfloat16),
            pltpu.VMEM((2 * DEPTH, steps, width), jnp.bfloat16),
            pltpu.SMEM((requests,), jnp.int32),
            pltpu.SMEM((requests,), jnp.int32),
            pltpu.SMEM((16,), jnp.int32),
            pltpu.SemaphoreType.DMA((2,)),
            pltpu.SemaphoreType.DMA((2 * DEPTH,)),
            pltpu.SemaphoreType.DMA((2 * DEPTH,)),
        ]
        + score_scratch(kv, pages * own.shape[2], group * steps),
        compiler_params=pltpu.CompilerParams(vmem_limit_bytes=VMEM_LIMIT),
        cost_estimate=cost(12),
        name="local",
    )(lengths, target, table, queries, suffix, own, sib, ctx)


def far_kernel(
    chips, dims, first, rows, meta_ref, q_ref, own_ref, sib_ref, out_ref, pool, todo, keys, begin,
    row_at, ends, sem, *scores,
):
    requests, steps, kv, group, head, pages = dims
    core = lax.rem(lax.axis_index("replica"), 2)
    width = kv * group * head
    held = own_ref.shape[0]
    load_own, load_sib = load_pools(own_ref, sib_ref, pool, sem)
    load_own.start()
    load_sib.start()
    row_at[0] = 0

    def bounds(i):
        low = jnp.maximum(begin[i], 0)
        high = jnp.minimum(begin[i] + meta_ref[i, pages], rows)
        return low, high, (high - (low // 16) * 16 + 15) // 16

    def class_of(i):
        here = shift_of(meta_ref[i, pages + 1], chips) == 0
        row = row_at[0]
        row_at[0] = row + jnp.where(here, meta_ref[i, pages], 0)
        begin[i] = row - first
        low, high, need = bounds(i)
        mine = jnp.where(lax.rem(meta_ref[i, pages + 1], 2) == core, 0, 3) + 3 - need
        return jnp.where(here & (high > low), mine, 6)

    arrange(requests, 7, class_of, keys, ends, todo)
    owned, count = ends[2], ends[5]
    out_ref[...] = jnp.zeros_like(out_ref)

    def compute(picked, window):
        items, spans, lives = [], [], []
        for i in picked:
            low, high, _ = bounds(i)
            base = pl.multiple_of(jnp.minimum((low // 16) * 16, rows - window), 16)
            span = pl.ds(base, window)
            row = base + lax.broadcasted_iota(jnp.int32, (window, STAT), 0)
            shift = jnp.where(lax.rem(meta_ref[i, pages + 1], 2) == core, 0, held)
            ids = [meta_ref[i, p] + shift for p in range(pages)]
            items.append((q_ref[span, :], ids, None))
            spans.append(span)
            lives.append((row >= low) & (row < high))
        found = attend(items, dims, window, pool, scores)
        for u, (span, live) in enumerate(zip(spans, lives)):
            for k in range(kv):
                for g in range(group):
                    cut = slice((k * group + g) * head, (k * group + g + 1) * head)
                    old = out_ref[span, cut].astype(jnp.float32)
                    part = found[u][k][0][g * window : (g + 1) * window]
                    out_ref[span, cut] = jnp.where(live, part, old).astype(jnp.bfloat16)
            old = out_ref[span, width : width + STAT].astype(jnp.float32)
            new = split_stat(found[u], group, window)
            out_ref[span, width : width + STAT] = jnp.where(live, new, old).astype(jnp.bfloat16)

    load_own.wait()

    @pl.when(owned == count)
    def _():
        load_sib.wait()

    def step(pair, carry):
        @pl.when((owned < count) & (pair == owned // 2))
        def _():
            load_sib.wait()

        picked = [todo[2 * pair], todo[jnp.minimum(2 * pair + 1, count - 1)]]
        need = jnp.maximum(bounds(picked[0])[2], bounds(picked[1])[2])
        for blocks in (1, 2, 3):
            if 16 * blocks <= rows:

                @pl.when(need == blocks)
                def _():
                    compute(picked, 16 * blocks)

        return carry

    lax.fori_loop(0, (count + 1) // 2, step, 0)


def far(chunk, meta, own, sib, dims, chips, first):
    rows, width = chunk.shape
    requests, steps, kv, group, head, pages = dims
    held = own.shape[0]
    return pl.pallas_call(
        functools.partial(far_kernel, chips, dims, first, rows),
        in_specs=[sspec(), vspec(), anyspec(), anyspec()],
        out_specs=vspec(),
        out_shape=jax.ShapeDtypeStruct((rows, width + STAT), jnp.bfloat16),
        scratch_shapes=[
            pltpu.VMEM((2 * held,) + own.shape[1:], jnp.bfloat16),
            pltpu.SMEM((requests,), jnp.int32),
            pltpu.SMEM((requests,), jnp.int32),
            pltpu.SMEM((requests,), jnp.int32),
            pltpu.SMEM((1,), jnp.int32),
            pltpu.SMEM((16,), jnp.int32),
            pltpu.SemaphoreType.DMA((2,)),
        ]
        + score_scratch(kv, pages * own.shape[2], group * min(48, rows)),
        compiler_params=pltpu.CompilerParams(vmem_limit_bytes=VMEM_LIMIT),
        cost_estimate=cost(6),
        name="far",
    )(meta, chunk, own, sib)


def merge_kernel(
    chips, dims, chunk, len_ref, dst_ref, old_ref, stat_ref, back_hbm, ctx_ref, back_ref, tiles, got,
    hot, todo, begin, take_sem, give_sem, back_sem,
):
    requests, steps, kv, group, head, pages = dims
    way, first, rows = chunk
    heads = kv * group
    width = heads * head
    many = got.shape[0] // steps
    back = pltpu.make_async_copy(back_hbm, back_ref, back_sem)
    back.start()
    count = flow(
        chips, requests, way, first, rows, lambda i: len_ref[i], lambda i: dst_ref[i], todo, begin
    )

    def take(j):
        return pltpu.make_async_copy(old_ref.at[todo[j]], tiles.at[j], take_sem.at[j])

    def give(j):
        return pltpu.make_async_copy(tiles.at[j], ctx_ref.at[todo[j]], give_sem.at[j])

    def issue(j, carry):
        take(j).start()
        return carry

    lax.fori_loop(0, count, issue, 0)
    back.wait()

    def whole(stat):
        return (
            stat
            + pltpu.roll(stat, STAT - heads, axis=1)
            + pltpu.roll(stat, STAT - 2 * heads, axis=1)
        )

    def some(j, u):
        picked = [jnp.minimum(j + n, count - 1) for n in range(4)]
        for n in range(4):

            @pl.when(j + n < count)
            def _():
                take(j + n).wait()

        for n, at in enumerate(picked):
            i = todo[at]
            span = pl.ds(pl.multiple_of((u + n) * steps, steps), steps)
            far_sum = whole(got[span, width : width + STAT])
            near_sum = whole(stat_ref[i].astype(jnp.float32))
            share = 1.0 / (1.0 + jnp.exp(near_sum - far_sum))
            token = lax.broadcasted_iota(jnp.int32, (steps, STAT), 0)
            here = begin[at] + token
            share = jnp.where((token < len_ref[i]) & (here >= 0) & (here < rows), share, 0.0)
            for h in range(heads):
                cut = slice(h * head, (h + 1) * head)
                near = tiles[j + n, :, cut].astype(jnp.float32)
                mixed = near + share[:, h : h + 1] * (got[span, cut] - near)
                tiles[j + n, :, cut] = mixed.astype(jnp.bfloat16)
        for n in range(4):

            @pl.when(j + n < count)
            def _():
                give(j + n).start()

    def block(b, carry):
        for u in range(many):
            j = jnp.minimum(b * many + u, count - 1)
            size = jnp.where(b * many + u < count, len_ref[todo[j]], 0)
            token = lax.broadcasted_iota(jnp.int32, (steps, rows), 0)
            row = lax.broadcasted_iota(jnp.int32, (steps, rows), 1)
            match = (begin[j] + token == row) & (token < size)
            hot[u * steps : (u + 1) * steps, :] = jnp.where(match, 1.0, 0.0).astype(jnp.bfloat16)
        got[...] = jnp.dot(hot[...], back_ref[...], preferred_element_type=jnp.float32)

        def each(quad, inner):
            some(b * many + quad * 4, quad * 4)
            return inner

        left = jnp.minimum(count - b * many, many)
        lax.fori_loop(0, (left + 3) // 4, each, 0)
        return carry

    lax.fori_loop(0, (count + many - 1) // many, block, 0)

    def drain(j, carry):
        give(j).wait()
        return carry

    lax.fori_loop(0, count, drain, 0)


def merge(ctx, stat, back, lengths, target, dims, chips, chunk, room):
    requests, steps, width = ctx.shape
    many = 8
    return pl.pallas_call(
        functools.partial(merge_kernel, chips, dims, chunk),
        in_specs=[sspec(), sspec(), anyspec(), vspec(), anyspec()],
        out_specs=anyspec(),
        out_shape=jax.ShapeDtypeStruct(ctx.shape, jnp.bfloat16),
        input_output_aliases={2: 0},
        scratch_shapes=[
            pltpu.VMEM(back.shape, jnp.bfloat16),
            pltpu.VMEM((-(-room // many) * many, steps, width), jnp.bfloat16),
            pltpu.VMEM((many * steps, width + STAT), jnp.float32),
            pltpu.VMEM((many * steps, chunk[2]), jnp.bfloat16),
            pltpu.SMEM((requests + 1,), jnp.int32),
            pltpu.SMEM((requests + 1,), jnp.int32),
            pltpu.SemaphoreType.DMA((room,)),
            pltpu.SemaphoreType.DMA((room,)),
            pltpu.SemaphoreType.DMA,
        ],
        compiler_params=pltpu.CompilerParams(vmem_limit_bytes=VMEM_LIMIT),
        cost_estimate=cost(3),
        name="merge",
    )(lengths, target, ctx, stat, back)


def shards(queries, suffix_key_value, kv_pool, page_table, lengths, destination):
    replicas = lax.axis_size("replica")
    chips = replicas // 2
    requests, steps, width = queries.shape
    kv, head = suffix_key_value.shape[2], suffix_key_value.shape[3] // 2
    pages = page_table.shape[1]
    dims = (requests, steps, kv, width // (kv * head), head, pages)
    target = destination[:, 0]
    here = lax.axis_index("replica") >> 1
    ways = range(1, chips)

    room = 2 * (requests // replicas + 1)
    most = room * steps
    mean = requests * steps // (2 * chips)
    base = min(most, -(-(mean * 3) // (4 * 32)) * 32)
    sizes = [most - base]
    if chips == 2:
        sizes = sorted({min(most, mean * n // 8) - base for n in (9, 10, 11, 12, 14)} - {0})
        sizes = [-(-size // 16) * 16 for size in sizes if size < most - base] + [most - base]

    def away(s):
        return [(r, (r + 2 * s) % replicas) for r in range(replicas)]

    def back(s):
        return [((r + 2 * s) % replicas, r) for r in range(replicas)]

    meta = jnp.concatenate([page_table, lengths[:, None], destination], axis=1)
    metas = {s: lax.ppermute(meta, "replica", away(s)) for s in ways}
    packed = [pack(queries, lengths, target, chips, (s, 0, base)) for s in ways]
    packed, metas = lax.optimization_barrier((packed, metas))
    arrived = [lax.ppermute(rows, "replica", away(s)) for s, rows in zip(ways, packed)]
    sib = lax.ppermute(kv_pool, "replica", [(r, r ^ 1) for r in range(replicas)])
    pool, sib, packed = lax.optimization_barrier((kv_pool, sib, packed))
    own = jnp.transpose(pool, (0, 2, 1, 3))
    sib = jnp.transpose(sib, (0, 2, 1, 3))
    suffix = jnp.transpose(suffix_key_value, (0, 2, 1, 3))

    def finish(size):
        def run():
            def serve(rows, s, first):
                out = far(rows, metas[s], own, sib, dims, chips, first)
                return out, lax.ppermute(out, "replica", back(s))

            more = [pack(queries, lengths, target, chips, (s, base, size)) for s in ways]
            more = [lax.ppermute(rows, "replica", away(s)) for s, rows in zip(ways, more)]
            first, came_first = zip(*[serve(r, s, 0) for s, r in zip(ways, arrived)])
            near_target, first = lax.optimization_barrier((target, first))
            ctx, stat = near_part(queries, suffix, lengths, near_target, dims, chips)
            stat, more = lax.optimization_barrier((stat, more))
            second, came_second = zip(*[serve(r, s, base) for s, r in zip(ways, more)])
            ctx, second = lax.optimization_barrier((ctx, second))
            ctx = local(queries, suffix, own, sib, ctx, page_table, lengths, target, dims, chips)
            for first_row, rows, came in ((0, base, came_first), (base, size, came_second)):
                for s, r in zip(ways, came):
                    chunk = (s, first_row, rows)
                    ctx = merge(ctx, stat, r, lengths, target, dims, chips, chunk, room)
            return ctx

        return run

    if len(sizes) == 1:
        return finish(sizes[0])()

    def flow_of(table, sender):
        goes = (table[:, pages + 1] >> 1) != sender
        return jnp.sum(jnp.where(goes, table[:, pages], 0))

    widest = jnp.maximum(flow_of(meta, here), flow_of(metas[1], 1 - here)).reshape(1)
    widest = jnp.maximum(
        widest, lax.ppermute(widest, "replica", [(r, r ^ 1) for r in range(replicas)])
    )
    seen = widest
    parts = lax.axis_size("groups")
    for hop in range(1, parts):
        other = lax.ppermute(seen, "groups", [(g, (g + hop) % parts) for g in range(parts)])
        widest = jnp.maximum(widest, other)
    level = sum((widest[0] > base + size).astype(jnp.int32) for size in sizes[:-1])
    return lax.switch(level, [finish(size) for size in sizes])


def solution(mesh):
    return jax.shard_map(
        shards,
        mesh=mesh,
        in_specs=(
            P(("groups", "replica"), None, "tensor"),
            P(("groups", "replica"), None, "tensor", None),
            P(("groups", "replica"), None, "tensor", None),
            P(("groups", "replica"), None),
            P(("groups", "replica")),
            P(("groups", "replica"), None),
        ),
        out_specs=P(("groups", "replica"), None, "tensor"),
        check_vma=False,
    )
```

profile of v0, /device:TPU:0, one launch (start us, length us, event | category | flops | bytes accessed | tf_op | source)
XLA Modules:
  0.0 143.5 jit_solution(11665851166690113436)
XLA Ops:
  0.0 0.0 copy-start.2
  0.0 0.0 copy-start.1
  0.0 0.0 copy-start.3
  0.0 5.2 %copy.34 = bf16[64,64,2,256]{3,1,2,0:T(8,128)(2,1)} copy(bf16[64,64,2,256]{3,2,1,0:T(2,128)(2,1)} %param.14) | data formatting | bytes 8388608 | tf_op args[2]
  5.2 0.0 copy-start
  5.2 0.5 collective-permute-start.22
  5.6 0.0 copy-done.2
  5.6 0.1 copy.32
  5.7 0.0 copy-done.1
  5.7 0.1 copy.31
  5.8 0.0 copy-done.3
  5.8 0.1 copy.33
  5.9 0.1 pad_add_fusion
  6.0 2.5 %collective-permute-start.18 = (s32[32,18]{1,0:T(8,128)S(1)}, s32[32,18]{1,0:T(8,128)S(1)}, u32[]{:S(2)}, u32[]{:S(2)}) collective-permute-start(s32[32,18]{1,0:T(8,128)S(1)} %pad_add_fusion), channel_id=1, source_target_pairs={{0,8},{4,12},{8,0},{12,4},{1,9},{5,13},{9,1},{13,5},{2,10},{6,14},... | collective-permute-start | bytes 6920 | tf_op jit(solution)/shard_map/ppermute | solution.py:765
  8.5 4.4 %pack.13 = bf16[192,2048]{1,0:T(8,128)(2,1)} custom-call(s32[32]{0:T(128)S(1)} %copy-done.2, s32[32]{0:T(128)S(1)} %bitcast.25, bf16[32,32,2048]{2,1,0:T(8,128)(2,1)} %q_ref.1), custom_call_target="tpu_custom_call" | custom-call | flops 1100000000 | bytes 1024 | tf_op jit(solution)/shard_map/pack/pallas_call | solution.py:117
  12.9 0.0 collective-permute-done.18
  12.9 0.1 collective-permute-start.21
  13.0 0.0 copy-done
  13.0 0.2 copy.46
  13.3 0.6 fusion
  13.9 0.7 select_reduce_fusion
  15.7 1.0 collective-permute-start.19
  16.6 0.2 collective-permute-done.19
  17.5 3.4 %collective-permute-start.20 = (s32[1]{0:T(128)}, s32[1]{0:T(128)}, u32[]{:S(2)}, u32[]{:S(2)}) collective-permute-start(s32[1]{0:T(128)} %max.10), channel_id=1, source_target_pairs={{0,16},{16,0},{1,17},{17,1},{2,18},{18,2},{3,19},{19,3},{4,20},{20... | collective-permute-start | bytes 20 | tf_op jit(solution)/shard_map/ppermute | solution.py:812
  20.9 0.2 collective-permute-done.20
  21.8 0.0 collective-permute-done.22
  21.8 5.1 %copy.45 = bf16[64,64,2,256]{3,1,2,0:T(8,128)(2,1)} copy(bf16[64,64,2,256]{3,2,1,0:T(2,128)(2,1)} %param.14) | data formatting | bytes 8388608 | tf_op jit(solution)/shard_map/optimization_barrier | solution.py:770
  27.0 5.7 %collective-permute-done.21 = bf16[192,2048]{1,0:T(8,128)(2,1)S(1)} collective-permute-done((bf16[192,2048]{1,0:T(8,128)(2,1)}, bf16[192,2048]{1,0:T(8,128)(2,1)S(1)}, u32[]{:S(2)}, u32[]{:S(2)}) %collective-permute-start.21) | collective-permute-done | bytes 786464 | tf_op jit(solution)/shard_map/ppermute | solution.py:768
  32.7 109.7 %conditional.1 = (bf16[32,32,2048]{2,1,0:T(8,128)(2,1)}) conditional(s32[]{:T(128)} %bitcast.3, (s32[32,18]{1,0:T(8,128)S(1)}, bf16[192,2048]{1,0:T(8,128)(2,1)S(1)}, bf16[64,2,64,256]{3,2,1,0:T(8,128)(2,1)}, bf16[64,2,64,256]{3,2,1,0:T(8,128)(2,1)}, s32[32]{0:T(128)S(1)}, /*index=5*/s32[32]{0:T(128)S(1)}, ...), branch_computations={%region_2.3_spmd, %region_3.4_spmd, %region_4.5_spmd, %region_5.6_... | conditional | flops 36299997184 | bytes 29306068 | solution.py:815
  53.9 4.4 %pack.9 = bf16[160,2048]{1,0:T(8,128)(2,1)} custom-call(s32[32]{0:T(128)S(1)} %get-tuple-element.150.len_ref, s32[32]{0:T(128)S(1)} %get-tuple-element.159.dst_ref, bf16[32,32,2048]{2,1,0:T(8,128)(2,1)} %get-tuple-element.153.q_ref), custom_call_target="tpu_custom_call" | custom-call | flops 1100000000 | bytes 1024 | tf_op jit(solution)/shard_map/cond/branch_2_fun/pack/pallas_call | solution.py:117
  58.4 0.7 collective-permute-start.6
  59.0 14.4 %far.16 = bf16[192,2176]{1,0:T(8,128)(2,1)} custom-call(s32[32,18]{1,0:T(8,128)S(1)} %get-tuple-element.157.meta_ref, bf16[192,2048]{1,0:T(8,128)(2,1)S(1)} %get-tuple-element.158.q_ref, bf16[64,2,64,256]{3,2,1,0:T(8,128)(2,1)} %get-tuple-element.155.own_ref, bf16[64,2,64,256]{3,2,1,0:T(8,128)(2,1)} %get-tuple-element.156.sib_ref), custom_call_target="tpu_custom_call" | custom-call | flops 6600000000 | bytes 1024 | tf_op jit(solution)/shard_map/cond/branch_2_fun/far/pallas_call | solution.py:601
  73.4 1.1 collective-permute-start.7
  74.5 0.7 copy.39.table_ref
  75.2 10.1 %near.8 = (bf16[32,32,2048]{2,1,0:T(8,128)(2,1)}, bf16[32,32,128]{2,1,0:T(8,128)(2,1)}) custom-call(s32[32]{0:T(128)S(1)} %get-tuple-element.150.len_ref, s32[32]{0:T(128)S(1)} %get-tuple-element.159.dst_ref, bf16[32,32,2048]{2,1,0:T(8,128)(2,1)} %get-tuple-element.153.q_ref, bf16[32,2,32,256]{3,2,1,0:T(8,128)(2,1)S(1)} %get-tuple-element.154.suf_ref), custom_call_target="tpu_custom_call" | custom-call | flops 2200000000 | bytes 1024 | tf_op jit(solution)/shard_map/cond/branch_2_fun/near/pallas_call | solution.py:366
  85.3 0.0 collective-permute-done.6.q_ref
  85.3 8.4 %far.17 = bf16[160,2176]{1,0:T(8,128)(2,1)} custom-call(s32[32,18]{1,0:T(8,128)S(1)} %get-tuple-element.157.meta_ref, bf16[160,2048]{1,0:T(8,128)(2,1)} %collective-permute-done.6.q_ref, bf16[64,2,64,256]{3,2,1,0:T(8,128)(2,1)} %get-tuple-element.155.own_ref, bf16[64,2,64,256]{3,2,1,0:T(8,128)(2,1)} %get-tuple-element.156.sib_ref), custom_call_target="tpu_custom_call" | custom-call | flops 6600000000 | bytes 1024 | tf_op jit(solution)/shard_map/cond/branch_2_fun/far/pallas_call | solution.py:601
  93.7 6.0 %collective-permute-start.8 = (bf16[160,2176]{1,0:T(8,128)(2,1)}, bf16[160,2176]{1,0:T(8,128)(2,1)S(1)}, u32[]{:S(2)}, u32[]{:S(2)}) collective-permute-start(bf16[160,2176]{1,0:T(8,128)(2,1)} %far.17), channel_id=1, source_target_pairs={{8,0},{12,4},{0,8},{4,12},{9,1},{13,5},{1,9},{5,13},{10,2},{14,6},... | collective-permute-start | bytes 2088968 | tf_op jit(solution)/shard_map/cond/branch_2_fun/ppermute | solution.py:779
  99.8 17.1 %local.8.old_ref = bf16[32,32,2048]{2,1,0:T(8,128)(2,1)} custom-call(s32[32]{0:T(128)S(1)} %get-tuple-element.150.len_ref, s32[32]{0:T(128)S(1)} %get-tuple-element.159.dst_ref, s32[32,16]{1,0:T(8,128)} %copy.39.table_ref, bf16[32,32,2048]{2,1,0:T(8,128)(2,1)} %get-tuple-element.153.q_ref, ...), custom_call_target="tpu_custom_call", output_to_operand_aliasing={{}: (7, {})} | custom-call | flops 13200000000 | bytes 1024 | tf_op jit(solution)/shard_map/cond/branch_2_fun/local/pallas_call | solution.py:493
  116.9 0.0 collective-permute-done.7.back_hbm
  116.9 0.0 copy-start.9
  116.9 0.9 copy-done.9
  117.8 6.9 %merge.16.old_ref = bf16[32,32,2048]{2,1,0:T(8,128)(2,1)} custom-call(s32[32]{0:T(128)S(1)} %get-tuple-element.150.len_ref, s32[32]{0:T(128)S(1)} %get-tuple-element.159.dst_ref, bf16[32,32,2048]{2,1,0:T(8,128)(2,1)} %local.8.old_ref, bf16[32,32,128]{2,1,0:T(8,128)(2,1)} %get-tuple-element.164.stat_ref, ...), custom_call_target="tpu_custom_call", output_to_operand_aliasing={{}: (2, {})} | custom-call | flops 3300000000 | bytes 1024 | tf_op jit(solution)/shard_map/cond/branch_2_fun/merge/pallas_call | solution.py:715
  124.7 0.0 collective-permute-done.8.back_hbm
  124.7 0.0 copy-start.15
  124.7 0.9 copy-done.15
  125.6 6.8 %merge.17 = bf16[32,32,2048]{2,1,0:T(8,128)(2,1)} custom-call(s32[32]{0:T(128)S(1)} %get-tuple-element.150.len_ref, s32[32]{0:T(128)S(1)} %get-tuple-element.159.dst_ref, bf16[32,32,2048]{2,1,0:T(8,128)(2,1)} %merge.16.old_ref, bf16[32,32,128]{2,1,0:T(8,128)(2,1)} %get-tuple-element.164.stat_ref, ...), custom_call_target="tpu_custom_call", output_to_operand_aliasing={{}: (2, {})} | custom-call | flops 3300000000 | bytes 1024 | tf_op jit(solution)/shard_map/cond/branch_2_fun/merge/pallas_call | solution.py:715
Async XLA Ops:
  0.0 5.6 %copy-start.2 = (s32[32]{0:T(128)S(1)}, s32[32]{0:T(128)}, u32[]{:S(2)}) copy-start(s32[32]{0:T(128)} %len_ref.1) | copy-start | bytes 388
  0.0 5.7 %copy-start.1 = (s32[32,16]{0,1:T(8,128)S(1)}, s32[32,16]{0,1:T(8,128)}, u32[]{:S(2)}) copy-start(s32[32,16]{0,1:T(8,128)} %param.15) | copy-start | bytes 6148
  0.0 5.8 %copy-start.3 = (s32[32,1]{0,1:T(1,128)S(1)}, s32[32,1]{0,1:T(1,128)}, u32[]{:S(2)}) copy-start(s32[32,1]{0,1:T(1,128)} %param.17) | copy-start | bytes 388
  5.2 7.8 %copy-start = (bf16[32,32,2,256]{3,2,1,0:T(2,128)(2,1)S(1)}, bf16[32,32,2,256]{3,2,1,0:T(2,128)(2,1)}, u32[]{:S(2)}) copy-start(bf16[32,32,2,256]{3,2,1,0:T(2,128)(2,1)} %param.13) | copy-start | bytes 3145732
  5.2 16.6 %collective-permute-start.22 = (bf16[64,64,2,256]{3,1,2,0:T(8,128)(2,1)}, bf16[64,64,2,256]{3,1,2,0:T(8,128)(2,1)}, u32[]{:S(2)}, u32[]{:S(2)}) collective-permute-start(bf16[64,64,2,256]{3,1,2,0:T(8,128)(2,1)} %copy.34), channel_id=1, source_target_pairs={{0,4},{4,0},{8,12},{12,8},{1,5},{5,1},{9,13},{13,9},{2,6},{6,2},{1... | collective-permute-start | bytes 12582920 | tf_op jit(solution)/shard_map/ppermute | solution.py:769
  6.0 7.0 %collective-permute-start.18 = (s32[32,18]{1,0:T(8,128)S(1)}, s32[32,18]{1,0:T(8,128)S(1)}, u32[]{:S(2)}, u32[]{:S(2)}) collective-permute-start(s32[32,18]{1,0:T(8,128)S(1)} %pad_add_fusion), channel_id=1, source_target_pairs={{0,8},{4,12},{8,0},{12,4},{1,9},{5,13},{9,1},{13,5},{2,10},{6,14},... | collective-permute-start | bytes 6920 | tf_op jit(solution)/shard_map/ppermute | solution.py:765
  12.9 19.8 %collective-permute-start.21 = (bf16[192,2048]{1,0:T(8,128)(2,1)}, bf16[192,2048]{1,0:T(8,128)(2,1)S(1)}, u32[]{:S(2)}, u32[]{:S(2)}) collective-permute-start(bf16[192,2048]{1,0:T(8,128)(2,1)} %pack.13), channel_id=1, source_target_pairs={{0,8},{4,12},{8,0},{12,4},{1,9},{5,13},{9,1},{13,5},{2,10},{6,14},... | collective-permute-start | bytes 2359304 | tf_op jit(solution)/shard_map/ppermute | solution.py:768
  15.7 1.2 collective-permute-start.19
  17.5 3.6 %collective-permute-start.20 = (s32[1]{0:T(128)}, s32[1]{0:T(128)}, u32[]{:S(2)}, u32[]{:S(2)}) collective-permute-start(s32[1]{0:T(128)} %max.10), channel_id=1, source_target_pairs={{0,16},{16,0},{1,17},{17,1},{2,18},{18,2},{3,19},{19,3},{4,20},{20... | collective-permute-start | bytes 20 | tf_op jit(solution)/shard_map/ppermute | solution.py:812
  58.4 27.0 %collective-permute-start.6 = (bf16[160,2048]{1,0:T(8,128)(2,1)}, bf16[160,2048]{1,0:T(8,128)(2,1)}, u32[]{:S(2)}, u32[]{:S(2)}) collective-permute-start(bf16[160,2048]{1,0:T(8,128)(2,1)} %pack.9), channel_id=1, source_target_pairs={{0,8},{4,12},{8,0},{12,4},{1,9},{5,13},{9,1},{13,5},{2,10},{6,14},... | collective-permute-start | bytes 1966088 | tf_op jit(solution)/shard_map/cond/branch_2_fun/ppermute | solution.py:782
  73.4 43.4 %collective-permute-start.7 = (bf16[192,2176]{1,0:T(8,128)(2,1)}, bf16[192,2176]{1,0:T(8,128)(2,1)S(1)}, u32[]{:S(2)}, u32[]{:S(2)}) collective-permute-start(bf16[192,2176]{1,0:T(8,128)(2,1)} %far.16), channel_id=1, source_target_pairs={{8,0},{12,4},{0,8},{4,12},{9,1},{13,5},{1,9},{5,13},{10,2},{14,6},... | collective-permute-start | bytes 2506760 | tf_op jit(solution)/shard_map/cond/branch_2_fun/ppermute | solution.py:779
  93.7 31.0 %collective-permute-start.8 = (bf16[160,2176]{1,0:T(8,128)(2,1)}, bf16[160,2176]{1,0:T(8,128)(2,1)S(1)}, u32[]{:S(2)}, u32[]{:S(2)}) collective-permute-start(bf16[160,2176]{1,0:T(8,128)(2,1)} %far.17), channel_id=1, source_target_pairs={{8,0},{12,4},{0,8},{4,12},{9,1},{13,5},{1,9},{5,13},{10,2},{14,6},... | collective-permute-start | bytes 2088968 | tf_op jit(solution)/shard_map/cond/branch_2_fun/ppermute | solution.py:779
  116.9 0.9 copy-start.9
  124.7 0.9 copy-start.15
where the time goes:
time: 145 us; the launch traced here: 143 us
  Pallas kernels  72.5 us (50%)
  loops' own time  31.3 us (22%)
  starting transfers between devices  15.2 us (10%)
  local copies, waits for them, and re-layouts  13.2 us (9%)
  waiting for transfers between devices  6.12 us (4%)
  between operations  3.69 us (3%)
    another operation x1, loops' own time, shards(): return lax.switch(level, [finish(size) for size in sizes])  31.3 us
    pallas_call x2, Pallas kernels, far(): pl.pallas_call(functools.partial(far_kernel, chips, dims, first, rows), i...  22.8 us
    pallas_call x1, Pallas kernels, local(): pl.pallas_call(functools.partial(local_kernel, chips, dims), in_specs=[ss...  17.1 us
    pallas_call x2, Pallas kernels, merge(): pl.pallas_call(functools.partial(merge_kernel, chips, dims, chunk), in_sp...  13.7 us
    pallas_call x1, Pallas kernels, near_part(): pl.pallas_call(functools.partial(near_kernel, chips, dims), in_specs=[ssp...  10.1 us
    pallas_call x2, Pallas kernels, pack(): pl.pallas_call(functools.partial(pack_kernel, chips, chunk, requests), in...  8.84 us
    ppermute x2, starting transfers between devices, serve(): return (out, lax.ppermute(out, 'replica', back(s)))  7.12 us
    ppermute x1, waiting for transfers between devices, shards(): lax.ppermute(rows, 'replica', away(s))  5.73 us
  transfers between devices with their start and end apart: 8, of which 3 were waited for; matrix products, arithmetic and copies ran while one was open for 5% of the time, Pallas kernels for 43%

commit v1 on v0

--- a/solution.py
+++ b/solution.py
@@ -94,17 +94,25 @@
         hot[...] = jnp.where(row == place, 1.0, 0.0).astype(jnp.bfloat16)
         for u in range(many):
             take(j, slot, u).wait()
-        block = tiles[slot].reshape(many * steps, width)
-        rows_of = jnp.dot(hot[...], block, preferred_element_type=jnp.float32).astype(jnp.bfloat16)
-
-        @pl.when(j == 0)
-        def _():
-            out_ref[...] = rows_of
-
-        @pl.when(j > 0)
-        def _():
-            out_ref[...] += rows_of
-
+
+        def column(c, inner):
+            cut = pl.ds(pl.multiple_of(c * 256, 256), 256)
+            block = tiles[slot, :, :, cut].reshape(many * steps, 256)
+            rows_of = jnp.dot(hot[...], block, preferred_element_type=jnp.float32)
+
+            @pl.when(j > 0)
+            def _():
+                out_ref[:, cut] = (out_ref[:, cut].astype(jnp.float32) + rows_of).astype(
+                    jnp.bfloat16
+                )
+
+            @pl.when(j == 0)
+            def _():
+                out_ref[:, cut] = rows_of.astype(jnp.bfloat16)
+
+            return inner
+
+        lax.fori_loop(0, width // 256, column, 0)
         return carry
 
     lax.fori_loop(0, blocks, step, 0)
@@ -140,67 +148,45 @@
     return jnp.concatenate([values, jnp.ones_like(values)], axis=1)
 
 
-def stacked(q, k, group, head):
-    return jnp.concatenate(
-        [q[:, (k * group + g) * head : (k * group + g + 1) * head] for g in range(group)], axis=0
-    )
-
-
-def attend(items, dims, window, pool, scores):
+def attend(q, k, dims, window, pool, ids, suffix, s_ref, p_ref):
     requests, steps, kv, group, head, pages = dims
     coeff = 1.0 / math.sqrt(head)
     rows = group * window
-    per = pool.shape[2]
-    count = 4 if pages % 4 == 0 else 1
-    work = [(n, k) for n in range(len(items)) for k in range(kv)]
-    s_refs = dict(zip(work, scores[: len(work)]))
-    p_refs = dict(zip(work, scores[len(work) :]))
-    if items[0][2] is not None:
+    qk = jnp.concatenate([q[:, g * head : (g + 1) * head] for g in range(group)], axis=0)
+    near = None
+    if suffix is not None:
         key = lax.broadcasted_iota(jnp.int32, (window, steps), 1)
         token = lax.broadcasted_iota(jnp.int32, (window, steps), 0)
         causal = jnp.where(key <= token, 0.0, -1e30)
-        causal = jnp.concatenate([causal] * group, axis=0)
-    nears = {}
-    for n, k in work:
-        q, ids, suffix = items[n]
-        qk = stacked(q, k, group, head)
+        near = nt_dot(qk, suffix[k, :, 0:head]) + jnp.concatenate([causal] * group, axis=0)
+    if pool is None:
+        top = jnp.max(near, axis=1, keepdims=True)
+        mixed = None
+    else:
+        per = pool.shape[2]
+        count = 4 if pages % 4 == 0 else 1
         for p in range(0, pages, count):
             keys = jnp.concatenate([pool[i, k, :, 0:head] for i in ids[p : p + count]], axis=0)
-            s_refs[n, k][0:rows, p * per : (p + count) * per] = nt_dot(qk, keys)
-        if suffix is not None:
-            nears[n, k] = nt_dot(qk, suffix[k, :, 0:head]) + causal
-    tops = {}
-    for n, k in work:
+            s_ref[0:rows, p * per : (p + count) * per] = nt_dot(qk, keys)
         found = []
         for r in range(0, rows, 16):
-            score = s_refs[n, k][r : r + 16, :]
+            score = s_ref[r : r + 16, :]
             top = jnp.max(score, axis=1, keepdims=True)
-            if (n, k) in nears:
-                near = nears[n, k][r : r + 16]
-                top = jnp.maximum(top, jnp.max(near, axis=1, keepdims=True))
-            p_refs[n, k][r : r + 16, :] = jnp.exp((score - top) * coeff).astype(jnp.bfloat16)
+            if near is not None:
+                top = jnp.maximum(top, jnp.max(near[r : r + 16], axis=1, keepdims=True))
+            p_ref[r : r + 16, :] = jnp.exp((score - top) * coeff).astype(jnp.bfloat16)
             found.append(top)
-        tops[n, k] = jnp.concatenate(found, axis=0)
-    mixes = {}
-    for n, k in work:
-        q, ids, suffix = items[n]
+        top = jnp.concatenate(found, axis=0)
         values = jnp.concatenate([pool[i, k, :, head : 2 * head] for i in ids], axis=0)
-        mixed = jnp.dot(
-            p_refs[n, k][0:rows, :], with_ones(values), preferred_element_type=jnp.float32
+        mixed = jnp.dot(p_ref[0:rows, :], with_ones(values), preferred_element_type=jnp.float32)
+    if near is not None:
+        weight = jnp.exp((near - top) * coeff).astype(jnp.bfloat16)
+        more = jnp.dot(
+            weight, with_ones(suffix[k, :, head : 2 * head]), preferred_element_type=jnp.float32
         )
-        if suffix is not None:
-            weight = jnp.exp((nears[n, k] - tops[n, k]) * coeff).astype(jnp.bfloat16)
-            mixed += jnp.dot(
-                weight,
-                with_ones(suffix[k, :, head : 2 * head]),
-                preferred_element_type=jnp.float32,
-            )
-        mixes[n, k] = mixed
-    results = [[None] * kv for _ in items]
-    for n, k in work:
-        total = mixes[n, k][:, head : 2 * head]
-        results[n][k] = (mixes[n, k][:, 0:head] * inverse(total), tops[n, k] * coeff, total)
-    return results
+        mixed = more if mixed is None else mixed + more
+    total = mixed[:, head : 2 * head]
+    return mixed[:, 0:head] * inverse(total), top * coeff, total
 
 
 def inverse(total):
@@ -208,25 +194,25 @@
     return share * (2.0 - total * share)
 
 
-def split_stat(values, group, window):
+def note_stat(level_ref, total_ref, k, group, window, top, total):
     lane = lax.broadcasted_iota(jnp.int32, (window, STAT), 1)
-    count = len(values) * group
-    assert count & (count - 1) == 0
-    which = lane & (count - 1)
-    level = jnp.zeros((window, STAT), jnp.float32)
-    total = jnp.ones((window, STAT), jnp.float32)
-    for k, (_, top, weight) in enumerate(values):
-        for g in range(group):
-            here = which == k * group + g
-            level = jnp.where(here, top[g * window : (g + 1) * window], level)
-            total = jnp.where(here, weight[g * window : (g + 1) * window, 0:STAT], total)
-    stat = level + jnp.log(total)
+    level, weight = level_ref[0:window, :], total_ref[0:window, :]
+    for g in range(group):
+        here = lane == k * group + g
+        level = jnp.where(here, top[g * window : (g + 1) * window], level)
+        weight = jnp.where(here, total[g * window : (g + 1) * window, 0:STAT], weight)
+    level_ref[0:window, :] = level
+    total_ref[0:window, :] = weight
+
+
+def split_stat(level, total, count):
+    lane = lax.broadcasted_iota(jnp.int32, level.shape, 1)
+    stat = jnp.where(lane < count, level + jnp.log(jnp.where(lane < count, total, 1.0)), 0.0)
     high = stat.astype(jnp.bfloat16).astype(jnp.float32)
     rest = stat - high
     middle = rest.astype(jnp.bfloat16).astype(jnp.float32)
     low = rest - middle
-    stat = jnp.where(lane < count, high, jnp.where(lane < 2 * count, middle, low))
-    return jnp.where(lane < 3 * count, stat, 0.0)
+    return high + pltpu.roll(middle, count, axis=1) + pltpu.roll(low, 2 * count, axis=1)
 
 
 def load_pools(own_ref, sib_ref, pool, sem):
@@ -262,19 +248,18 @@
 
 
 def score_scratch(kv, keys, rows):
-    return [pltpu.VMEM((rows, keys), jnp.float32) for _ in range(2 * kv)] + [
-        pltpu.VMEM((rows, keys), jnp.bfloat16) for _ in range(2 * kv)
-    ]
+    return [pltpu.VMEM((rows, keys), jnp.float32), pltpu.VMEM((rows, keys), jnp.bfloat16)]
 
 
 BATCH = 4
 
 
 def near_kernel(
-    chips, dims, len_ref, dst_ref, q_ref, suf_ref, ctx_ref, stat_ref, q_buf, o_buf, todo, q_sem, o_sem
+    chips, dims, len_ref, dst_ref, q_ref, suf_ref, ctx_ref, stat_ref, q_buf, o_buf, level, total,
+    todo, q_sem, o_sem,
 ):
     requests, steps, kv, group, head, pages = dims
-    coeff = 1.0 / math.sqrt(head)
+    span = group * head
 
     def listing(i, count):
         todo[count] = i
@@ -302,13 +287,6 @@
 
     each(0, take, "start")
     stat_ref[...] = jnp.zeros_like(stat_ref)
-    key = lax.broadcasted_iota(jnp.int32, (steps, BATCH * steps), 1)
-    token = lax.broadcasted_iota(jnp.int32, (steps, BATCH * steps), 0)
-    masks = []
-    for u in range(BATCH):
-        mine = (key >= u * steps) & (key - u * steps <= token)
-        masks.append(jnp.concatenate([jnp.where(mine, 0.0, -1e30)] * group, axis=0))
-
     def step(block, carry):
         slot = lax.rem(block, 2)
         each(block + 1, take, "start")
@@ -317,38 +295,30 @@
             each(block - 2, give, "wait")
 
         each(block, take, "wait")
-        picked = [todo[jnp.minimum(block * BATCH + u, count - 1)] for u in range(BATCH)]
-        found = []
-        for k in range(kv):
-            keys = jnp.concatenate([suf_ref[i, k, :, 0:head] for i in picked], axis=0)
-            found.append(
-                [
-                    nt_dot(stacked(q_buf[slot, u], k, group, head), keys) + masks[u]
-                    for u in range(BATCH)
-                ]
-            )
-        tops = [[jnp.max(score, axis=1, keepdims=True) for score in scores] for scores in found]
-        for u in range(BATCH):
-            i = picked[u]
+
+        def one(u, carry):
+            i = todo[block * BATCH + u]
             live = lax.broadcasted_iota(jnp.int32, (steps, head), 0) < len_ref[i]
-            values = []
-            for k in range(kv):
-                rows = jnp.concatenate([suf_ref[n, k, :, head : 2 * head] for n in picked], axis=0)
-                weight = jnp.exp((found[k][u] - tops[k][u]) * coeff).astype(jnp.bfloat16)
-                mixed = jnp.dot(weight, with_ones(rows), preferred_element_type=jnp.float32)
-                total = mixed[:, head : 2 * head]
-                mixed = mixed[:, 0:head] * inverse(total)
-                values.append((None, tops[k][u] * coeff, total))
+
+            def part(k, inner):
+                at = pl.multiple_of(k * span, span)
+                mixed, top, weight = attend(
+                    q_buf[slot, u, :, pl.ds(at, span)], k, dims, steps, None, None,
+                    suf_ref.at[i], None, None,
+                )
                 for g in range(group):
-                    h = k * group + g
-                    part = jnp.where(live, mixed[g * steps : (g + 1) * steps], 0.0)
-                    o_buf[slot, u, :, h * head : (h + 1) * head] = part.astype(jnp.bfloat16)
-            stat = split_stat(values, group, steps).astype(jnp.bfloat16)
-
-            @pl.when(block * BATCH + u < count)
-            def _():
-                stat_ref[i] = stat
-
+                    piece = jnp.where(live, mixed[g * steps : (g + 1) * steps], 0.0)
+                    cut = pl.ds(pl.multiple_of(at + g * head, head), head)
+                    o_buf[slot, u, :, cut] = piece.astype(jnp.bfloat16)
+                note_stat(level, total, k, group, steps, top, weight)
+                return inner
+
+            lax.fori_loop(0, kv, part, 0)
+            stat = split_stat(level[0:steps, :], total[0:steps, :], kv * group)
+            stat_ref[i] = stat.astype(jnp.bfloat16)
+            return carry
+
+        lax.fori_loop(0, jnp.minimum(count - block * BATCH, BATCH), one, 0)
         each(block, give, "start")
         return carry
 
@@ -374,6 +344,8 @@
         scratch_shapes=[
             pltpu.VMEM((2, BATCH, steps, width), jnp.bfloat16),
             pltpu.VMEM((2, BATCH, steps, width), jnp.bfloat16),
+            pltpu.VMEM((steps, STAT), jnp.float32),
+            pltpu.VMEM((steps, STAT), jnp.float32),
             pltpu.SMEM((requests + 1,), jnp.int32),
             pltpu.SemaphoreType.DMA((2, BATCH)),
             pltpu.SemaphoreType.DMA((2, BATCH)),
@@ -426,26 +398,29 @@
     for ahead in range(DEPTH - 1):
         each(ahead, take, "start")
 
-    def compute(pair, picked, window):
-        slots = [2 * lax.rem(pair, DEPTH) + u for u in range(2)]
-        items = []
-        for u, i in enumerate(picked):
-            shift = jnp.where(lax.rem(dst_ref[i], 2) == core, 0, held)
-            ids = [table_ref[i, p] + shift for p in range(pages)]
-            items.append((q_buf[slots[u], 0:window, :], ids, suf_ref.at[i]))
-        found = attend(items, dims, window, pool, scores)
-        for u, i in enumerate(picked):
-            live = lax.broadcasted_iota(jnp.int32, (window, head), 0) < len_ref[i]
-            for k in range(kv):
-                for g in range(group):
-                    h = k * group + g
-                    part = found[u][k][0][g * window : (g + 1) * window]
-                    part = jnp.where(live, part, 0.0).astype(jnp.bfloat16)
-                    o_buf[slots[u], 0:window, h * head : (h + 1) * head] = part
-            if window < steps:
-                o_buf[slots[u], window:steps, :] = jnp.zeros(
-                    (steps - window, o_buf.shape[2]), jnp.bfloat16
-                )
+    def compute(slot, i, window):
+        shift = jnp.where(lax.rem(dst_ref[i], 2) == core, 0, held)
+        ids = [table_ref[i, p] + shift for p in range(pages)]
+        live = lax.broadcasted_iota(jnp.int32, (window, head), 0) < len_ref[i]
+        span = group * head
+
+        def part(k, inner):
+            at = pl.multiple_of(k * span, span)
+            mixed, _, _ = attend(
+                q_buf[slot, 0:window, pl.ds(at, span)], k, dims, window, pool, ids,
+                suf_ref.at[i], *scores,
+            )
+            for g in range(group):
+                piece = jnp.where(live, mixed[g * window : (g + 1) * window], 0.0)
+                cut = pl.ds(pl.multiple_of(at + g * head, head), head)
+                o_buf[slot, 0:window, cut] = piece.astype(jnp.bfloat16)
+            return inner
+
+        lax.fori_loop(0, kv, part, 0)
+        if window < steps:
+            o_buf[slot, window:steps, :] = jnp.zeros(
+                (steps - window, o_buf.shape[2]), jnp.bfloat16
+            )
 
     load_own.wait()
 
@@ -465,15 +440,20 @@
             load_sib.wait()
 
         each(pair, take, "wait")
-        picked = [todo[2 * pair], todo[jnp.minimum(2 * pair + 1, count - 1)]]
-        size = jnp.maximum(len_ref[picked[0]], len_ref[picked[1]])
-        need = (size + quarter - 1) // quarter
-        for quarters in (1, 2, 3, 4):
-
-            @pl.when(need == quarters)
-            def _():
-                compute(pair, picked, quarter * quarters)
-
+
+        def one(u, inner):
+            i = todo[2 * pair + u]
+            slot = 2 * lax.rem(pair, DEPTH) + u
+            need = (len_ref[i] + steps // 2 - 1) // (steps // 2)
+            for halves in (1, 2):
+
+                @pl.when(need == halves)
+                def _():
+                    compute(slot, i, halves * (steps // 2))
+
+            return inner
+
+        lax.fori_loop(0, jnp.minimum(count - 2 * pair, 2), one, 0)
         each(pair, give, "start")
         return carry
 
@@ -515,8 +495,8 @@
 
 
 def far_kernel(
-    chips, dims, first, rows, meta_ref, q_ref, own_ref, sib_ref, out_ref, pool, todo, keys, begin,
-    row_at, ends, sem, *scores,
+    chips, dims, first, rows, meta_ref, q_ref, own_ref, sib_ref, out_ref, pool, level, total, todo,
+    keys, begin, row_at, ends, sem, *scores,
 ):
     requests, steps, kv, group, head, pages = dims
     core = lax.rem(lax.axis_index("replica"), 2)
@@ -545,29 +525,33 @@
     owned, count = ends[2], ends[5]
     out_ref[...] = jnp.zeros_like(out_ref)
 
-    def compute(picked, window):
-        items, spans, lives = [], [], []
-        for i in picked:
-            low, high, _ = bounds(i)
-            base = pl.multiple_of(jnp.minimum((low // 16) * 16, rows - window), 16)
-            span = pl.ds(base, window)
-            row = base + lax.broadcasted_iota(jnp.int32, (window, STAT), 0)
-            shift = jnp.where(lax.rem(meta_ref[i, pages + 1], 2) == core, 0, held)
-            ids = [meta_ref[i, p] + shift for p in range(pages)]
-            items.append((q_ref[span, :], ids, None))
-            spans.append(span)
-            lives.append((row >= low) & (row < high))
-        found = attend(items, dims, window, pool, scores)
-        for u, (span, live) in enumerate(zip(spans, lives)):
-            for k in range(kv):
-                for g in range(group):
-                    cut = slice((k * group + g) * head, (k * group + g + 1) * head)
-                    old = out_ref[span, cut].astype(jnp.float32)
-                    part = found[u][k][0][g * window : (g + 1) * window]
-                    out_ref[span, cut] = jnp.where(live, part, old).astype(jnp.bfloat16)
-            old = out_ref[span, width : width + STAT].astype(jnp.float32)
-            new = split_stat(found[u], group, window)
-            out_ref[span, width : width + STAT] = jnp.where(live, new, old).astype(jnp.bfloat16)
+    def compute(i, window):
+        low, high, _ = bounds(i)
+        base = pl.multiple_of(jnp.minimum((low // 16) * 16, rows - window), 16)
+        span = pl.ds(base, window)
+        row = base + lax.broadcasted_iota(jnp.int32, (window, STAT), 0)
+        live = (row >= low) & (row < high)
+        shift = jnp.where(lax.rem(meta_ref[i, pages + 1], 2) == core, 0, held)
+        ids = [meta_ref[i, p] + shift for p in range(pages)]
+        wide = group * head
+
+        def part(k, inner):
+            at = pl.multiple_of(k * wide, wide)
+            mixed, top, weight = attend(
+                q_ref[span, pl.ds(at, wide)], k, dims, window, pool, ids, None, *scores
+            )
+            for g in range(group):
+                cut = pl.ds(pl.multiple_of(at + g * head, head), head)
+                old = out_ref[span, cut].astype(jnp.float32)
+                piece = jnp.where(live, mixed[g * window : (g + 1) * window], old)
+                out_ref[span, cut] = piece.astype(jnp.bfloat16)
+            note_stat(level, total, k, group, window, top, weight)
+            return inner
+
+        lax.fori_loop(0, kv, part, 0)
+        old = out_ref[span, width : width + STAT].astype(jnp.float32)
+        new = split_stat(level[0:window, :], total[0:window, :], kv * group)
+        out_ref[span, width : width + STAT] = jnp.where(live, new, old).astype(jnp.bfloat16)
 
     load_own.wait()
 
@@ -575,23 +559,23 @@
     def _():
         load_sib.wait()
 
-    def step(pair, carry):
-        @pl.when((owned < count) & (pair == owned // 2))
+    def step(j, carry):
+        @pl.when(j == owned)
         def _():
             load_sib.wait()
 
-        picked = [todo[2 * pair], todo[jnp.minimum(2 * pair + 1, count - 1)]]
-        need = jnp.maximum(bounds(picked[0])[2], bounds(picked[1])[2])
+        i = todo[j]
+        need = bounds(i)[2]
         for blocks in (1, 2, 3):
             if 16 * blocks <= rows:
 
                 @pl.when(need == blocks)
                 def _():
-                    compute(picked, 16 * blocks)
-
-        return carry
-
-    lax.fori_loop(0, (count + 1) // 2, step, 0)
+                    compute(i, 16 * blocks)
+
+        return carry
+
+    lax.fori_loop(0, count, step, 0)
 
 
 def far(chunk, meta, own, sib, dims, chips, first):
@@ -605,6 +589,8 @@
         out_shape=jax.ShapeDtypeStruct((rows, width + STAT), jnp.bfloat16),
         scratch_shapes=[
             pltpu.VMEM((2 * held,) + own.shape[1:], jnp.bfloat16),
+            pltpu.VMEM((48, STAT), jnp.float32),
+            pltpu.VMEM((48, STAT), jnp.float32),
             pltpu.SMEM((requests,), jnp.int32),
             pltpu.SMEM((requests,), jnp.int32),
             pltpu.SMEM((requests,), jnp.int32),
@@ -654,33 +640,22 @@
             + pltpu.roll(stat, STAT - 2 * heads, axis=1)
         )
 
-    def some(j, u):
-        picked = [jnp.minimum(j + n, count - 1) for n in range(4)]
-        for n in range(4):
-
-            @pl.when(j + n < count)
-            def _():
-                take(j + n).wait()
-
-        for n, at in enumerate(picked):
-            i = todo[at]
-            span = pl.ds(pl.multiple_of((u + n) * steps, steps), steps)
-            far_sum = whole(got[span, width : width + STAT])
-            near_sum = whole(stat_ref[i].astype(jnp.float32))
-            share = 1.0 / (1.0 + jnp.exp(near_sum - far_sum))
-            token = lax.broadcasted_iota(jnp.int32, (steps, STAT), 0)
-            here = begin[at] + token
-            share = jnp.where((token < len_ref[i]) & (here >= 0) & (here < rows), share, 0.0)
-            for h in range(heads):
-                cut = slice(h * head, (h + 1) * head)
-                near = tiles[j + n, :, cut].astype(jnp.float32)
-                mixed = near + share[:, h : h + 1] * (got[span, cut] - near)
-                tiles[j + n, :, cut] = mixed.astype(jnp.bfloat16)
-        for n in range(4):
-
-            @pl.when(j + n < count)
-            def _():
-                give(j + n).start()
+    def one(j, u):
+        i = todo[j]
+        span = pl.ds(pl.multiple_of(u * steps, steps), steps)
+        far_sum = whole(got[span, width : width + STAT])
+        near_sum = whole(stat_ref[i].astype(jnp.float32))
+        share = 1.0 / (1.0 + jnp.exp(near_sum - far_sum))
+        token = lax.broadcasted_iota(jnp.int32, (steps, STAT), 0)
+        here = begin[j] + token
+        share = jnp.where((token < len_ref[i]) & (here >= 0) & (here < rows), share, 0.0)
+        take(j).wait()
+        for h in range(heads):
+            cut = slice(h * head, (h + 1) * head)
+            near = tiles[j, :, cut].astype(jnp.float32)
+            mixed = near + share[:, h : h + 1] * (got[span, cut] - near)
+            tiles[j, :, cut] = mixed.astype(jnp.bfloat16)
+        give(j).start()
 
     def block(b, carry):
         for u in range(many):
@@ -690,14 +665,24 @@
             row = lax.broadcasted_iota(jnp.int32, (steps, rows), 1)
             match = (begin[j] + token == row) & (token < size)
             hot[u * steps : (u + 1) * steps, :] = jnp.where(match, 1.0, 0.0).astype(jnp.bfloat16)
-        got[...] = jnp.dot(hot[...], back_ref[...], preferred_element_type=jnp.float32)
-
-        def each(quad, inner):
-            some(b * many + quad * 4, quad * 4)
+
+        def column(c, inner):
+            cut = pl.ds(pl.multiple_of(c * 256, 256), 256)
+            got[:, cut] = jnp.dot(
+                hot[...], back_ref[:, cut], preferred_element_type=jnp.float32
+            )
             return inner
 
-        left = jnp.minimum(count - b * many, many)
-        lax.fori_loop(0, (left + 3) // 4, each, 0)
+        lax.fori_loop(0, width // 256, column, 0)
+        got[:, width : width + STAT] = jnp.dot(
+            hot[...], back_ref[:, width : width + STAT], preferred_element_type=jnp.float32
+        )
+
+        def each(u, inner):
+            one(b * many + u, u)
+            return inner
+
+        lax.fori_loop(0, jnp.minimum(count - b * many, many), each, 0)
         return carry
 
     lax.fori_loop(0, (count + many - 1) // many, block, 0)
@@ -752,7 +737,7 @@
     base = min(most, -(-(mean * 3) // (4 * 32)) * 32)
     sizes = [most - base]
     if chips == 2:
-        sizes = sorted({min(most, mean * n // 8) - base for n in (9, 10, 11, 12, 14)} - {0})
+        sizes = sorted({min(most, mean * n // 8) - base for n in (10, 12)} - {0})
         sizes = [-(-size // 16) * 16 for size in sizes if size < most - base] + [most - base]
 
     def away(s):
@@ -766,11 +751,11 @@
     packed = [pack(queries, lengths, target, chips, (s, 0, base)) for s in ways]
     packed, metas = lax.optimization_barrier((packed, metas))
     arrived = [lax.ppermute(rows, "replica", away(s)) for s, rows in zip(ways, packed)]
-    sib = lax.ppermute(kv_pool, "replica", [(r, r ^ 1) for r in range(replicas)])
-    pool, sib, packed = lax.optimization_barrier((kv_pool, sib, packed))
-    own = jnp.transpose(pool, (0, 2, 1, 3))
-    sib = jnp.transpose(sib, (0, 2, 1, 3))
+    own = jnp.transpose(kv_pool, (0, 2, 1, 3))
+    sib = lax.ppermute(own, "replica", [(r, r ^ 1) for r in range(replicas)])
     suffix = jnp.transpose(suffix_key_value, (0, 2, 1, 3))
+    near_target, packed = lax.optimization_barrier((target, packed))
+    begun, stat = near_part(queries, suffix, lengths, near_target, dims, chips)
 
     def finish(size):
         def run():
@@ -781,11 +766,9 @@
             more = [pack(queries, lengths, target, chips, (s, base, size)) for s in ways]
             more = [lax.ppermute(rows, "replica", away(s)) for s, rows in zip(ways, more)]
             first, came_first = zip(*[serve(r, s, 0) for s, r in zip(ways, arrived)])
-            near_target, first = lax.optimization_barrier((target, first))
-            ctx, stat = near_part(queries, suffix, lengths, near_target, dims, chips)
-            stat, more = lax.optimization_barrier((stat, more))
+            more, first = lax.optimization_barrier((more, first))
             second, came_second = zip(*[serve(r, s, base) for s, r in zip(ways, more)])
-            ctx, second = lax.optimization_barrier((ctx, second))
+            ctx, second = lax.optimization_barrier((begun, second))
             ctx = local(queries, suffix, own, sib, ctx, page_table, lengths, target, dims, chips)
             for first_row, rows, came in ((0, base, came_first), (base, size, came_second)):
                 for s, r in zip(ways, came):

time: 145 us -> 152 us (1.048)
  the two profiles are of different devices: /device:TPU:0 before, /device:TPU:6 now
where the time goes in v1:
time: 152 us; the launch traced here: 153 us
  Pallas kernels  124 us (82%)
  starting transfers between devices  14 us (9%)
  local copies, waits for them, and re-layouts  8.23 us (5%)
  between operations  2.82 us (2%)
  waiting for transfers between devices  1.83 us (1%)
    pallas_call x2, Pallas kernels, far(): pl.pallas_call(functools.partial(far_kernel, chips, dims, first, rows), i...  40.7 us
    pallas_call x1, Pallas kernels, local(): pl.pallas_call(functools.partial(local_kernel, chips, dims), in_specs=[ss...  40.4 us
    pallas_call x1, Pallas kernels, near_part(): pl.pallas_call(functools.partial(near_kernel, chips, dims), in_specs=[ssp...  17 us
    pallas_call x2, Pallas kernels, merge(): pl.pallas_call(functools.partial(merge_kernel, chips, dims, chunk), in_sp...  14.5 us
    pallas_call x2, Pallas kernels, pack(): pl.pallas_call(functools.partial(pack_kernel, chips, chunk, requests), in...  11.7 us
    ppermute x2, starting transfers between devices, serve(): return (out, lax.ppermute(out, 'replica', back(s)))  5.96 us
    unnamed x12, local copies, waits for them, and re-layouts  5.49 us
    ppermute x1, starting transfers between devices, run(): lax.ppermute(rows, 'replica', away(s))  3.21 us
  transfers between devices with their start and end apart: 8, of which 1 were waited for; matrix products, arithmetic and copies ran while one was open for 2% of the time, Pallas kernels for 73%

profile of v1, /device:TPU:6, one launch (start us, length us, event | category | flops | bytes accessed | tf_op | source)
XLA Modules:
  0.0 153.1 jit_solution(15788584433102353564)
XLA Ops:
  0.0 0.0 copy-start.2
  0.0 0.0 copy-start.1
  0.0 0.0 copy-start.3
  0.0 5.1 %copy.29 = bf16[64,64,2,256]{3,1,2,0:T(8,128)(2,1)} copy(bf16[64,64,2,256]{3,2,1,0:T(2,128)(2,1)} %param.11) | data formatting | bytes 8388608 | tf_op args[2]
  5.1 0.0 copy-start
  5.1 0.0 collective-permute-start.13
  5.1 0.0 copy-done.2
  5.1 0.1 copy.20
  5.2 0.0 copy-done.1
  5.2 0.1 copy.19
  5.3 0.0 copy-done.3
  5.3 0.1 copy.21
  5.4 0.1 pad_add_fusion
  5.5 0.5 collective-permute-start.9
  6.0 5.8 %pack.7 = bf16[192,2048]{1,0:T(8,128)(2,1)} custom-call(s32[32]{0:T(128)S(1)} %copy-done.2, s32[32]{0:T(128)S(1)} %bitcast.16, bf16[32,32,2048]{2,1,0:T(8,128)(2,1)} %q_ref.3), custom_call_target="tpu_custom_call" | custom-call | flops 1100000000 | bytes 1024 | tf_op jit(solution)/shard_map/pack/pallas_call | solution.py:125
  11.8 0.0 collective-permute-done.9
  11.8 1.4 collective-permute-start.12
  13.1 0.0 copy-done
  13.1 0.2 copy.30
  13.3 0.6 fusion
  14.0 0.7 select_reduce_fusion
  16.0 1.0 collective-permute-start.10
  17.0 17.0 %near.1 = (bf16[32,32,2048]{2,1,0:T(8,128)(2,1)}, bf16[32,32,128]{2,1,0:T(8,128)(2,1)}) custom-call(s32[32]{0:T(128)S(1)} %copy-done.2, s32[32]{0:T(128)S(1)} %bitcast.17, bf16[32,32,2048]{2,1,0:T(8,128)(2,1)} %q_ref.3, bf16[32,2,32,256]{3,2,1,0:T(8,128)(2,1)S(1)} %bitcast.11), custom_call_target="tpu_custom_call" | custom-call | flops 2200000000 | bytes 1024 | tf_op jit(solution)/shard_map/near/pallas_call | solution.py:336
  34.0 0.0 collective-permute-done.10
  34.6 1.9 %collective-permute-start.11 = (s32[1]{0:T(128)}, s32[1]{0:T(128)}, u32[]{:S(2)}, u32[]{:S(2)}) collective-permute-start(s32[1]{0:T(128)} %max.10), channel_id=1, source_target_pairs={{0,16},{16,0},{1,17},{17,1},{2,18},{18,2},{3,19},{19,3},{4,20},{20... | collective-permute-start | bytes 20 | tf_op jit(solution)/shard_map/ppermute | solution.py:795
  36.5 1.8 %collective-permute-done.11 = s32[1]{0:T(128)} collective-permute-done((s32[1]{0:T(128)}, s32[1]{0:T(128)}, u32[]{:S(2)}, u32[]{:S(2)}) %collective-permute-start.11) | collective-permute-done | bytes 36 | tf_op jit(solution)/shard_map/ppermute | solution.py:795
  39.0 0.0 collective-permute-done.12
  39.0 0.0 collective-permute-done.13
  39.0 113.9 %conditional.1 = (bf16[32,32,2048]{2,1,0:T(8,128)(2,1)}) conditional(s32[]{:T(128)} %bitcast.3, (s32[32]{0:T(128)S(1)}, s32[32]{0:T(128)S(1)}, bf16[32,32,2048]{2,1,0:T(8,128)(2,1)}, s32[32,18]{1,0:T(8,128)S(1)}, bf16[192,2048]{1,0:T(8,128)(2,1)S(1)}, /*index=5*/bf16[64,2,64,256]{3,2,1,0:T(8,128)(2,1)}, ...), branch_computations={%region_2.3_spmd, %region_3.4_spmd, %region_4.5_spmd} | conditional | flops 34099998720 | bytes 30353648 | solution.py:798
  39.0 5.9 %pack.5 = bf16[192,2048]{1,0:T(8,128)(2,1)} custom-call(s32[32]{0:T(128)S(1)} %get-tuple-element.88.len_ref, s32[32]{0:T(128)S(1)} %get-tuple-element.89.dst_ref, bf16[32,32,2048]{2,1,0:T(8,128)(2,1)} %get-tuple-element.91.q_ref), custom_call_target="tpu_custom_call" | custom-call | flops 1100000000 | bytes 1024 | tf_op jit(solution)/shard_map/cond/branch_1_fun/pack/pallas_call | solution.py:125
  44.9 3.2 %collective-permute-start.3 = (bf16[192,2048]{1,0:T(8,128)(2,1)}, bf16[192,2048]{1,0:T(8,128)(2,1)}, u32[]{:S(2)}, u32[]{:S(2)}) collective-permute-start(bf16[192,2048]{1,0:T(8,128)(2,1)} %pack.5), channel_id=1, source_target_pairs={{0,8},{4,12},{8,0},{12,4},{1,9},{5,13},{9,1},{13,5},{2,10},{6,14},... | collective-permute-start | bytes 2359304 | tf_op jit(solution)/shard_map/cond/branch_1_fun/ppermute | solution.py:767
  48.1 30.3 %far.8 = bf16[192,2176]{1,0:T(8,128)(2,1)} custom-call(s32[32,18]{1,0:T(8,128)S(1)} %get-tuple-element.96.meta_ref, bf16[192,2048]{1,0:T(8,128)(2,1)S(1)} %get-tuple-element.97.q_ref, bf16[64,2,64,256]{3,2,1,0:T(8,128)(2,1)} %get-tuple-element.93.own_ref, bf16[64,2,64,256]{3,2,1,0:T(8,128)(2,1)} %get-tuple-element.94.sib_ref), custom_call_target="tpu_custom_call" | custom-call | flops 6600000000 | bytes 1024 | tf_op jit(solution)/shard_map/cond/branch_1_fun/far/pallas_call | solution.py:585
  78.5 0.1 collective-permute-start.4
  78.5 0.7 copy.25.table_ref
  79.2 0.0 collective-permute-done.3.q_ref
  79.2 10.4 %far.9 = bf16[192,2176]{1,0:T(8,128)(2,1)} custom-call(s32[32,18]{1,0:T(8,128)S(1)} %get-tuple-element.96.meta_ref, bf16[192,2048]{1,0:T(8,128)(2,1)} %collective-permute-done.3.q_ref, bf16[64,2,64,256]{3,2,1,0:T(8,128)(2,1)} %get-tuple-element.93.own_ref, bf16[64,2,64,256]{3,2,1,0:T(8,128)(2,1)} %get-tuple-element.94.sib_ref), custom_call_target="tpu_custom_call" | custom-call | flops 6600000000 | bytes 1024 | tf_op jit(solution)/shard_map/cond/branch_1_fun/far/pallas_call | solution.py:585
  89.6 5.9 %collective-permute-start.5 = (bf16[192,2176]{1,0:T(8,128)(2,1)}, bf16[192,2176]{1,0:T(8,128)(2,1)S(1)}, u32[]{:S(2)}, u32[]{:S(2)}) collective-permute-start(bf16[192,2176]{1,0:T(8,128)(2,1)} %far.9), channel_id=1, source_target_pairs={{8,0},{12,4},{0,8},{4,12},{9,1},{13,5},{1,9},{5,13},{10,2},{14,6},... | collective-permute-start | bytes 2506760 | tf_op jit(solution)/shard_map/cond/branch_1_fun/ppermute | solution.py:764
  95.5 0.0 copy-start.13
  95.5 40.4 %local.4.old_ref = bf16[32,32,2048]{2,1,0:T(8,128)(2,1)} custom-call(s32[32]{0:T(128)S(1)} %get-tuple-element.88.len_ref, s32[32]{0:T(128)S(1)} %get-tuple-element.89.dst_ref, s32[32,16]{1,0:T(8,128)} %copy.25.table_ref, bf16[32,32,2048]{2,1,0:T(8,128)(2,1)} %get-tuple-element.91.q_ref, ...), custom_call_target="tpu_custom_call", output_to_operand_aliasing={{}: (7, {})} | custom-call | flops 13200000000 | bytes 1024 | tf_op jit(solution)/shard_map/cond/branch_1_fun/local/pallas_call | solution.py:473
  135.9 0.0 collective-permute-done.4.back_hbm
  135.9 0.0 copy-start.6
  135.9 1.0 copy-done.6
  136.9 0.0 copy-done.13
  136.9 8.6 %merge.8.old_ref = bf16[32,32,2048]{2,1,0:T(8,128)(2,1)} custom-call(s32[32]{0:T(128)S(1)} %get-tuple-element.88.len_ref, s32[32]{0:T(128)S(1)} %get-tuple-element.89.dst_ref, bf16[32,32,2048]{2,1,0:T(8,128)(2,1)} %local.4.old_ref, bf16[32,32,128]{2,1,0:T(8,128)(2,1)S(1)} %copy-done.13, bf16[192,2176]{1,0:T(8,128)(2,1)} %copy-done.6), custom_call_target="tpu_custom_call", output_to_operand_aliasing={{}: (2, {})} | custom-call | flops 3300000000 | bytes 1024 | tf_op jit(solution)/shard_map/cond/branch_1_fun/merge/pallas_call | solution.py:700
  145.5 0.0 collective-permute-done.5.back_hbm
  145.5 0.0 copy-start.8
  145.5 1.0 copy-done.8
  146.5 5.9 %merge.9 = bf16[32,32,2048]{2,1,0:T(8,128)(2,1)} custom-call(s32[32]{0:T(128)S(1)} %get-tuple-element.88.len_ref, s32[32]{0:T(128)S(1)} %get-tuple-element.89.dst_ref, bf16[32,32,2048]{2,1,0:T(8,128)(2,1)} %merge.8.old_ref, bf16[32,32,128]{2,1,0:T(8,128)(2,1)S(1)} %copy-done.13, bf16[192,2176]{1,0:T(8,128)(2,1)} %copy-done.8), custom_call_target="tpu_custom_call", output_to_operand_aliasing={{}: (2, {})} | custom-call | flops 3300000000 | bytes 1024 | tf_op jit(solution)/shard_map/cond/branch_1_fun/merge/pallas_call | solution.py:700
Async XLA Ops:
  0.0 5.1 %copy-start.2 = (s32[32]{0:T(128)S(1)}, s32[32]{0:T(128)}, u32[]{:S(2)}) copy-start(s32[32]{0:T(128)} %len_ref.3) | copy-start | bytes 388
  0.0 5.2 %copy-start.1 = (s32[32,16]{0,1:T(8,128)S(1)}, s32[32,16]{0,1:T(8,128)}, u32[]{:S(2)}) copy-start(s32[32,16]{0,1:T(8,128)} %param.12) | copy-start | bytes 6148
  0.0 5.3 %copy-start.3 = (s32[32,1]{0,1:T(1,128)S(1)}, s32[32,1]{0,1:T(1,128)}, u32[]{:S(2)}) copy-start(s32[32,1]{0,1:T(1,128)} %param.14) | copy-start | bytes 388
  5.1 8.0 %copy-start = (bf16[32,32,2,256]{3,2,1,0:T(2,128)(2,1)S(1)}, bf16[32,32,2,256]{3,2,1,0:T(2,128)(2,1)}, u32[]{:S(2)}) copy-start(bf16[32,32,2,256]{3,2,1,0:T(2,128)(2,1)} %param.10) | copy-start | bytes 3145732
  5.1 33.8 %collective-permute-start.13 = (bf16[64,2,64,256]{3,2,1,0:T(8,128)(2,1)}, bf16[64,2,64,256]{3,2,1,0:T(8,128)(2,1)}, u32[]{:S(2)}, u32[]{:S(2)}) collective-permute-start(bf16[64,2,64,256]{3,2,1,0:T(8,128)(2,1)} %bitcast.9), channel_id=1, source_target_pairs={{0,4},{4,0},{8,12},{12,8},{1,5},{5,1},{9,13},{13,9},{2,6},{6,2},{1... | collective-permute-start | bytes 12582920 | tf_op jit(solution)/shard_map/ppermute | solution.py:755
  5.5 6.3 %collective-permute-start.9 = (s32[32,18]{1,0:T(8,128)S(1)}, s32[32,18]{1,0:T(8,128)S(1)}, u32[]{:S(2)}, u32[]{:S(2)}) collective-permute-start(s32[32,18]{1,0:T(8,128)S(1)} %pad_add_fusion), channel_id=1, source_target_pairs={{0,8},{4,12},{8,0},{12,4},{1,9},{5,13},{9,1},{13,5},{2,10},{6,14},... | collective-permute-start | bytes 6920 | tf_op jit(solution)/shard_map/ppermute | solution.py:750
  11.8 27.2 %collective-permute-start.12 = (bf16[192,2048]{1,0:T(8,128)(2,1)}, bf16[192,2048]{1,0:T(8,128)(2,1)S(1)}, u32[]{:S(2)}, u32[]{:S(2)}) collective-permute-start(bf16[192,2048]{1,0:T(8,128)(2,1)} %pack.7), channel_id=1, source_target_pairs={{0,8},{4,12},{8,0},{12,4},{1,9},{5,13},{9,1},{13,5},{2,10},{6,14},... | collective-permute-start | bytes 2359304 | tf_op jit(solution)/shard_map/ppermute | solution.py:753
  16.0 18.0 %collective-permute-start.10 = (s32[1]{0:T(128)}, s32[1]{0:T(128)}, u32[]{:S(2)}, u32[]{:S(2)}) collective-permute-start(s32[1]{0:T(128)} %bitcast.2), channel_id=1, source_target_pairs={{0,4},{4,0},{8,12},{12,8},{1,5},{5,1},{9,13},{13,9},{2,6},{6,2},{1... | collective-permute-start | bytes 20 | tf_op jit(solution)/shard_map/ppermute | solution.py:790
  34.6 3.7 %collective-permute-start.11 = (s32[1]{0:T(128)}, s32[1]{0:T(128)}, u32[]{:S(2)}, u32[]{:S(2)}) collective-permute-start(s32[1]{0:T(128)} %max.10), channel_id=1, source_target_pairs={{0,16},{16,0},{1,17},{17,1},{2,18},{18,2},{3,19},{19,3},{4,20},{20... | collective-permute-start | bytes 20 | tf_op jit(solution)/shard_map/ppermute | solution.py:795
  44.9 34.3 %collective-permute-start.3 = (bf16[192,2048]{1,0:T(8,128)(2,1)}, bf16[192,2048]{1,0:T(8,128)(2,1)}, u32[]{:S(2)}, u32[]{:S(2)}) collective-permute-start(bf16[192,2048]{1,0:T(8,128)(2,1)} %pack.5), channel_id=1, source_target_pairs={{0,8},{4,12},{8,0},{12,4},{1,9},{5,13},{9,1},{13,5},{2,10},{6,14},... | collective-permute-start | bytes 2359304 | tf_op jit(solution)/shard_map/cond/branch_1_fun/ppermute | solution.py:767
  78.5 57.5 %collective-permute-start.4 = (bf16[192,2176]{1,0:T(8,128)(2,1)}, bf16[192,2176]{1,0:T(8,128)(2,1)S(1)}, u32[]{:S(2)}, u32[]{:S(2)}) collective-permute-start(bf16[192,2176]{1,0:T(8,128)(2,1)} %far.8), channel_id=1, source_target_pairs={{8,0},{12,4},{0,8},{4,12},{9,1},{13,5},{1,9},{5,13},{10,2},{14,6},... | collective-permute-start | bytes 2506760 | tf_op jit(solution)/shard_map/cond/branch_1_fun/ppermute | solution.py:764
  89.6 55.9 %collective-permute-start.5 = (bf16[192,2176]{1,0:T(8,128)(2,1)}, bf16[192,2176]{1,0:T(8,128)(2,1)S(1)}, u32[]{:S(2)}, u32[]{:S(2)}) collective-permute-start(bf16[192,2176]{1,0:T(8,128)(2,1)} %far.9), channel_id=1, source_target_pairs={{8,0},{12,4},{0,8},{4,12},{9,1},{13,5},{1,9},{5,13},{10,2},{14,6},... | collective-permute-start | bytes 2506760 | tf_op jit(solution)/shard_map/cond/branch_1_fun/ppermute | solution.py:764
  95.5 41.5 %copy-start.13 = (bf16[32,32,128]{2,1,0:T(8,128)(2,1)S(1)}, bf16[32,32,128]{2,1,0:T(8,128)(2,1)}, u32[]{:S(2)}) copy-start(bf16[32,32,128]{2,1,0:T(8,128)(2,1)} %get-tuple-element.100.stat_ref) | copy-start | bytes 786436 | tf_op jit(solution)/shard_map/cond
  135.9 1.0 copy-start.6
  145.5 1.0 copy-start.8
